TPU v7x, 512 devices: a whole 4x4x16 slice. The times are simulated.
512 devices in a mesh: users: 32 (over y, x, core), items: 16 (over z).
Axes of the slice: x: 4, y: 4, z: 16, core: 2. Of those that a mesh axis runs over, the one named last changes fastest.
Arguments:
- user_emb: bfloat16 [65536, 256], P('users'), may hold values from -0.375 to 0.375
- samples: int32 [512, 64], P('users'), may hold values from 0 to 127, as said below
- pos_item: int32 [65536], P('users'), may hold values from 0 to 16383
- item_feat: bfloat16 [16384, 1024], P(('items', 'users')), may hold values from -0.1875 to 0.1875
- tower_w: bfloat16 [1024, 256], replicated, may hold values from -5 to 5
- item_bias: bfloat16 [16384], P(('items', 'users')), may hold values from -4 to 352
Outputs:
- user_loss: float32 [65536], P('users')
- user_grad: float32 [65536, 256], P(('users', 'items'))
- weight_grad: float32 [1024, 256], replicated
Inputs may be any that keep to these rules, and one draw needn't show every extreme that they name: `samples`: each row lists 64 distinct cluster ids. Clusters k * 8 to (k + 1) * 8 - 1 form item shard k; at most 8 ids of one row fall in any one shard, and in every row some shard holds exactly 8 of them.
All inputs are finite; a program needn't handle non-finite values.
Results may differ from a plain program's by a relative error of at most 0.0036.
Values may be sent and summed in bfloat16 or wider, within the bound.
No kernel may reach another device: no remote copies, remote signals or barrier semaphores. Data moves between devices by JAX's collectives and lax.ppermute only.
A program may use at most 64 MiB of HBM per device.

v0:
```python
import jax
import jax.numpy as jnp
from jax import lax
from jax.sharding import PartitionSpec as P

CL = 128
BU = 128
PEAK = 8
NEG_FILL = -1e30


def body(user_emb, samples, pos_item, item_feat, tower_w, item_bias):
    shard_index = lax.axis_index("items")
    group_size = lax.axis_size("users")
    shard_rows = item_feat.shape[0] * group_size
    shard_clus = shard_rows // CL
    slot_count = min(PEAK, shard_clus)
    shard_feats, bias_rows = (
        lax.all_gather(item_feat, "users", axis=0, tiled=True),
        lax.all_gather(item_bias, "users", axis=0, tiled=True),
    )
    item_rows = jnp.dot(shard_feats, tower_w, preferred_element_type=jnp.float32).astype(
        jnp.bfloat16
    )
    emb_width = item_rows.shape[1]
    emb_tiles = item_rows.reshape(shard_clus, CL, emb_width)
    bias_float = bias_rows.astype(jnp.float32)
    bias_tiles = bias_float.reshape(shard_clus, CL)
    blocks = samples.shape[0]
    step_count = blocks // 4
    local_ids = samples - shard_index * shard_clus
    inside = (local_ids >= 0) & (local_ids < shard_clus)
    rank_in = jnp.cumsum(inside.astype(jnp.int32), axis=1) - 1
    slot_range = jnp.arange(slot_count, dtype=jnp.int32)
    matched = inside[:, None, :] & (rank_in[:, None, :] == slot_range[None, :, None])
    slot_ids = jnp.sum(jnp.where(matched, local_ids[:, None, :], 0), axis=2)
    slot_live = jnp.any(matched, axis=2)
    pos_local = pos_item - shard_index * shard_rows
    pos_live = (pos_local >= 0) & (pos_local < shard_rows)
    pos_index = jnp.clip(pos_local, 0, shard_rows - 1)
    pos_rows = item_rows[pos_index]
    pos_logit = (
        jnp.einsum("ud,ud->u", user_emb, pos_rows, preferred_element_type=jnp.float32)
        + bias_float[pos_index]
    )
    user_steps = user_emb.reshape(step_count, 4, BU, emb_width)
    slot_steps = slot_ids.reshape(step_count, 4, slot_count)
    live_steps = slot_live.reshape(step_count, 4, slot_count)
    pos_steps = pos_logit.reshape(step_count, 4, BU)
    plive_steps = pos_live.reshape(step_count, 4, BU)

    def scores_of(user_rows, cluster_ids, live_ids):
        picked = emb_tiles[cluster_ids]
        raw_scores = jnp.einsum(
            "gud,gkcd->gukc", user_rows, picked, preferred_element_type=jnp.float32
        )
        raw_scores = raw_scores + bias_tiles[cluster_ids][:, None]
        live_mask = jnp.broadcast_to(live_ids[:, None, :, None], raw_scores.shape)
        return (picked, jnp.where(live_mask, raw_scores, NEG_FILL), live_mask)

    def forward(inputs):
        user_rows, cluster_ids, live_ids, pos_part, pos_flag = inputs
        picked, raw_scores, live_mask = scores_of(user_rows, cluster_ids, live_ids)
        row_peak = jnp.maximum(
            jnp.max(raw_scores, axis=(2, 3)), jnp.where(pos_flag, pos_part, NEG_FILL)
        )
        exp_total = jnp.sum(
            jnp.where(live_mask, jnp.exp(raw_scores - row_peak[..., None, None]), 0.0), axis=(2, 3)
        )
        exp_total = exp_total + jnp.where(pos_flag, jnp.exp(pos_part - row_peak), 0.0)
        return (row_peak, exp_total)

    local_peak, local_total = lax.map(
        forward, (user_steps, slot_steps, live_steps, pos_steps, plive_steps)
    )
    local_peak = local_peak.reshape(-1)
    local_total = local_total.reshape(-1)
    pos_value = jnp.where(pos_live, pos_logit, 0.0)
    row_peak = lax.pmax(local_peak, "items")
    exp_total, pos_score = lax.psum(
        (local_total * jnp.exp(local_peak - row_peak), pos_value), "items"
    )
    log_total = row_peak + jnp.log(exp_total)
    user_loss = log_total - pos_score
    pos_weight = jnp.where(pos_live, jnp.exp(pos_logit - log_total) - 1.0, 0.0)

    def weights_of(user_rows, cluster_ids, live_ids, log_part):
        picked, raw_scores, live_mask = scores_of(user_rows, cluster_ids, live_ids)
        soft_weight = jnp.where(
            live_mask, jnp.exp(raw_scores - log_part[..., None, None]), 0.0
        ).astype(jnp.bfloat16)
        return (picked, soft_weight)

    def add_tiles(grad_tiles, user_rows, cluster_ids, live_ids, soft_weight):
        contrib = jnp.einsum(
            "gukc,gud->gkcd", soft_weight, user_rows, preferred_element_type=jnp.float32
        )
        contrib = jnp.where(live_ids[..., None, None], contrib, 0.0)
        return grad_tiles.at[cluster_ids.reshape(-1)].add(contrib.reshape(-1, CL, emb_width))

    def backward_both(grad_tiles, inputs):
        user_rows, cluster_ids, live_ids, log_part = inputs
        picked, soft_weight = weights_of(user_rows, cluster_ids, live_ids, log_part)
        grad_users = jnp.einsum(
            "gukc,gkcd->gud", soft_weight, picked, preferred_element_type=jnp.float32
        )
        return (add_tiles(grad_tiles, user_rows, cluster_ids, live_ids, soft_weight), grad_users)

    start_tiles = jnp.zeros((shard_clus, CL, emb_width), jnp.float32)
    scan_inputs = (user_steps, slot_steps, live_steps, log_total.reshape(step_count, 4, BU))
    pos_terms = pos_weight[:, None] * pos_rows.astype(jnp.float32)
    grad_tiles, grad_users = lax.scan(backward_both, start_tiles, scan_inputs)
    grad_users = grad_users.reshape(-1, emb_width) + pos_terms
    user_grad = lax.psum_scatter(grad_users, "items", scatter_dimension=0, tiled=True)
    grad_items = (
        grad_tiles.reshape(shard_rows, emb_width)
        .at[pos_index]
        .add(pos_weight[:, None] * user_emb.astype(jnp.float32))
    )
    contract = (((0,), (0,)), ((), ()))
    part_weight = lax.dot_general(
        shard_feats.astype(jnp.float32), grad_items, contract, precision=lax.Precision.HIGHEST
    )
    weight_grad = lax.psum(part_weight, ("users", "items"))
    return (user_loss, user_grad, weight_grad)


def solution(mesh):
    return jax.shard_map(
        body,
        mesh=mesh,
        in_specs=(
            P("users", None),
            P("users", None),
            P("users"),
            P(("items", "users"), None),
            P(),
            P(("items", "users")),
        ),
        out_specs=(P("users"), P(("users", "items"), None), P()),
        check_vma=False,
    )
```

profile of v0, /device:TPU:4, one launch (start us, length us, event | category | flops | bytes accessed | tf_op | source)
XLA Modules:
  0.0 829.6 jit_solution(18017372859213118122)
XLA Ops:
  11.7 58.1 %all-reduce = bf16[1024]{0:T(1024)(128)(2,1)S(1)} all-reduce(bf16[1024]{0:T(1024)(128)(2,1)S(1)} %dynamic-update-slice), channel_id=1, replica_groups=mesh['users'=32,'items'=16] {'users'}, use_global_device_ids=true, to_apply=%add | all-reduce | flops 1024 | bytes 4096
  70.5 8.6 %gather_fusion.5 = f32[2048]{0:T(1024)S(1)} fusion(f32[1024]{0:T(1024)S(1)} %get-tuple-element.174, s32[2048]{0:T(1024)S(1)} %get-tuple-element.164), kind=kCustom, calls=%fused_computation.5 | custom fusion | bytes 24576 | tf_op jit(solution)/shard_map/gather | solution.py:44
  79.9 2.3 convolution_convert_fusion
  82.2 7.5 gather_fusion.4
  90.7 17.9 %while.24 = (s32[]{:T(128)}, f32[4,4,128]{2,1,0:T(4,128)S(1)}, f32[4,4,128]{2,1,0:T(4,128)S(1)}, pred[4,4,8]{2,1,0:T(4,128)(4,1)S(1)}, bf16[4,4,128,256]{3,2,1,0...) while((s32[]{:T(128)}, f32[4,4,128]{2,1,0:T(4,128)S(1)}, ...), condition=%wide.region_6.7_spmd, body=%wide.region_3.6_spmd.sunk | while | flops 272633440 | bytes 15036589 | solution.py:73
  92.1 1.9 fusion.43
  96.5 1.9 fusion.43
  108.6 36.2 %pmax.7 = f32[2048]{0:T(1024)S(1)} all-reduce(f32[2048]{0:T(1024)S(1)} %bitcast.148), channel_id=1, replica_groups=mesh['users'=32,'items'=16] {'items'}, use_global_device_ids=true, to_apply=%region_7.8 | all-reduce | flops 2048 | bytes 16384 | tf_op jit(solution)/shard_map/pmax | solution.py:79
  144.7 52.7 %all-reduce.1 = (f32[2048]{0:T(1024)S(1)}, f32[2048]{0:T(1024)S(1)}) all-reduce(f32[2048]{0:T(1024)S(1)} %exponential_multiply_fusion, f32[2048]{0:T(1024)S(1)} %get-tuple-element.161), channel_id=1, replica_groups=mesh['users'=32,'items'=16] {'items'}, use_global_device_ids=true, to_apply=%region_8.9 | all-reduce | flops 4096 | bytes 32768 | tf_op jit(solution)/shard_map/psum | solution.py:80
  197.5 64.0 %while.25 = (s32[]{:T(128)}, f32[8,128,256]{2,1,0:T(8,128)S(1)}, f32[4,4,128,256]{3,2,1,0:T(8,128)}, s32[4,4,8]{2,1,0:T(4,128)S(1)}, pred[4,4,8]{2,1,0:T(4,128)(...) while((s32[]{:T(128)}, f32[8,128,256]{2,1,0:T(8,128)S(1)}, ...), condition=%wide.region_12.13_spmd, body=%wide.region_10.12_spmd.sunk | while | flops 810026176 | bytes 42005372 | solution.py:112
  198.3 2.0 gather_fusion.2
  200.4 2.6 select_convert_fusion.2
  204.3 2.8 convolution_select_fusion.2
  207.1 6.4 scatter_fusion
  214.3 2.0 gather_fusion.2
  216.4 2.6 select_convert_fusion.2
  220.3 2.8 convolution_select_fusion.2
  223.1 6.5 scatter_fusion
  230.4 2.0 gather_fusion.2
  232.4 2.6 select_convert_fusion.2
  236.3 2.8 convolution_select_fusion.2
  239.1 6.5 scatter_fusion
  246.3 2.0 gather_fusion.2
  248.4 2.6 select_convert_fusion.2
  252.3 2.8 convolution_select_fusion.2
  255.1 6.5 scatter_fusion
  261.5 15.9 %scatter_custom_fusion.1 = f32[1024,256]{1,0:T(8,128)S(1)} fusion(f32[1024,256]{1,0:T(8,128)S(1)} %bitcast.128, s32[2048]{0:T(1024)S(1)} %get-tuple-element.165, bf16[2048,256]{1,0:T(8,128)(2,1)} %bitcast.137, f32[2048]{0:T(1024)S(1)} %get-tuple-element.159), kind=kCustom, calls=%fused_computation.46 | custom fusion | flops 1572864 | bytes 2105344 | tf_op jit(solution)/shard_map/scatter-add | solution.py:118
  277.4 4.5 convolution_bitcast_fusion.1
  282.0 3.3 fusion.17
  286.0 462.6 %all-reduce.4.cloned.1.call-done = f32[1024,256]{0,1:T(8,128)} async-done(((f32[1024,256]{0,1:T(8,128)}), f32[1024,256]{0,1:T(8,128)}) %all-reduce.4.cloned.1.call-update) | async-done | bytes 1048592 | tf_op jit(solution)/shard_map/psum | solution.py:124
  748.6 2.5 copy.14
  751.1 72.0 %reduce-scatter.2.cloned.1.call-done = f32[128,256]{1,0:T(8,128)} async-done(((f32[2048,256]{1,0:T(8,128)}), f32[128,256]{1,0:T(8,128)}) %reduce-scatter.2.cloned.1.call-update) | async-done | bytes 131088 | tf_op jit(solution)/shard_map/reduce_scatter | solution.py:114
  (134 shorter events, 29.3 us)
Async XLA Ops:
  7.2 72.7 %copy-start = (bf16[1024,256]{1,0:T(8,128)(2,1)S(1)}, bf16[1024,256]{1,0:T(8,128)(2,1)}, u32[]{:S(2)}) copy-start(bf16[1024,256]{1,0:T(8,128)(2,1)} %param.14) | copy-start | bytes 1572868
  7.2 72.7 %all-gather.2.cloned.1.call-start = ((), (), s32[]{:S(2)}) async-start(), calls=%async_computation.1 | async-start | bytes 2162688 | tf_op jit(solution)/shard_map/all_gather | solution.py:19
  7.9 740.7 %all-reduce.4.cloned.1.call-start = ((), (), s32[]{:S(2)}) async-start(), calls=%async_computation.3 | async-start | bytes 2097152 | tf_op jit(solution)/shard_map/psum | solution.py:124
  82.2 7.5 copy-start.2
  89.7 1.0 copy-start.5
  89.7 0.7 copy-start.7
  93.9 1.2 copy-start.3
  98.4 1.2 copy-start.3
  102.9 1.2 copy-start.3
  107.3 1.2 copy-start.3
  198.3 2.0 copy-start.4
  200.4 2.6 copy-start.1
  214.3 2.0 copy-start.4
  216.4 2.6 copy-start.1
  230.4 2.0 copy-start.4
  232.4 2.6 copy-start.1
  246.3 2.0 copy-start.4
  248.4 2.6 copy-start.1
  277.4 4.6 copy-start.6
  282.0 541.1 %reduce-scatter.2.cloned.1.call-start = ((), (), s32[]{:S(2)}) async-start(), calls=%async_computation.2 | async-start | bytes 2228224 | tf_op jit(solution)/shard_map/reduce_scatter | solution.py:114
Sparse Core Ops, SparseCore 0:
  11.1 63.0 all-gather.1
  282.1 466.4 all-reduce.3
  752.0 71.0 reduce-scatter.1
where the time goes:
time: 831 us; the launch traced here: 830 us
  waiting for transfers between devices  535 us (64%)
  blocking collectives  147 us (18%)
  other arithmetic  51.7 us (6%)
  matrix products  40.9 us (5%)
  local copies, waits for them, and re-layouts  39.6 us (5%)
  between operations  14.6 us (2%)
    psum x1, waiting for transfers between devices, body(): weight_grad = lax.psum(part_weight, ('users', 'items'))  463 us
    reduce_scatter x1, waiting for transfers between devices, body(): lax.psum_scatter(grad_users, 'items', scatter_dimension=0, tiled=True)  72 us
    unnamed x1, blocking collectives  58.1 us
    psum x1, blocking collectives, body(): lax.psum((local_total * jnp.exp(local_peak - row_peak), pos_value), 'items')  52.7 us
    pmax x1, blocking collectives, body(): row_peak = lax.pmax(local_peak, 'items')  36.2 us
    scatter-add x4, other arithmetic, add_tiles(): grad_tiles.at[cluster_ids.reshape(-1)]  25.8 us
    dot_general x8, matrix products, scores_of(): jnp.einsum('gud,gkcd->gukc', user_rows, picked, preferred_element_type=jn...  17.9 us
  transfers between devices with their start and end apart: 3, of which 2 were waited for; matrix products, arithmetic and copies ran while one was open for 2% of the time, Pallas kernels for 0%

commit v1 on v0

--- a/solution.py
+++ b/solution.py
@@ -121,7 +121,7 @@
     part_weight = lax.dot_general(
         shard_feats.astype(jnp.float32), grad_items, contract, precision=lax.Precision.HIGHEST
     )
-    weight_grad = lax.psum(part_weight, ("users", "items"))
+    weight_grad = lax.psum(lax.psum(part_weight, "items"), "users")
     return (user_loss, user_grad, weight_grad)
 
 

time: 831 us -> 640 us (0.77)
  the two profiles are of different devices: /device:TPU:4 before, /device:TPU:10 now
where the time goes in v1:
time: 640 us; the launch traced here: 639 us
  waiting for transfers between devices  351 us (55%)
  blocking collectives  141 us (22%)
  other arithmetic  51.7 us (8%)
  matrix products  40.8 us (6%)
  local copies, waits for them, and re-layouts  39.6 us (6%)
  between operations  14.6 us (2%)
    psum x2, waiting for transfers between devices, body(): weight_grad = lax.psum(lax.psum(part_weight, 'items'), 'users')  275 us
    reduce_scatter x1, waiting for transfers between devices, body(): lax.psum_scatter(grad_users, 'items', scatter_dimension=0, tiled=True)  75.5 us
    psum x1, blocking collectives, body(): lax.psum((local_total * jnp.exp(local_peak - row_peak), pos_value), 'items')  52.7 us
    unnamed x1, blocking collectives  51.3 us
    pmax x1, blocking collectives, body(): row_peak = lax.pmax(local_peak, 'items')  37.1 us
    scatter-add x4, other arithmetic, add_tiles(): grad_tiles.at[cluster_ids.reshape(-1)]  25.8 us
    dot_general x8, matrix products, scores_of(): jnp.einsum('gud,gkcd->gukc', user_rows, picked, preferred_element_type=jn...  17.9 us
    scatter-add x1, other arithmetic, body(): grad_items = grad_tiles.reshape(shard_rows, emb_width).at[pos_index].add(...  15.8 us
  transfers between devices with their start and end apart: 4, of which 3 were waited for; matrix products, arithmetic and copies ran while one was open for 3% of the time, Pallas kernels for 0%

profile of v1, /device:TPU:10, one launch (start us, length us, event | category | flops | bytes accessed | tf_op | source)
XLA Modules:
  0.0 639.4 jit_solution(6098991924400169564)
XLA Ops:
  11.7 51.3 %all-reduce = bf16[1024]{0:T(1024)(128)(2,1)S(1)} all-reduce(bf16[1024]{0:T(1024)(128)(2,1)S(1)} %dynamic-update-slice), channel_id=1, replica_groups=mesh['users'=32,'items'=16] {'users'}, use_global_device_ids=true, to_apply=%add | all-reduce | flops 1024 | bytes 4096
  63.7 8.6 %gather_fusion.5 = f32[2048]{0:T(1024)S(1)} fusion(f32[1024]{0:T(1024)S(1)} %get-tuple-element.174, s32[2048]{0:T(1024)S(1)} %get-tuple-element.164), kind=kCustom, calls=%fused_computation.5 | custom fusion | bytes 24576 | tf_op jit(solution)/shard_map/gather | solution.py:44
  73.1 2.3 convolution_convert_fusion
  75.4 7.5 %gather_fusion.4 = bf16[2048,256]{1,0:T(8,128)(2,1)S(1)} fusion(bf16[1024,256]{1,0:T(8,128)(2,1)S(1)} %convolution_convert_fusion, s32[2048]{0:T(1024)S(1)} %get-tuple-element.164), kind=kCustom, calls=%fused_computation.4 | custom fusion | bytes 2105344 | tf_op jit(solution)/shard_map/gather | solution.py:41
  83.9 17.9 %while.24 = (s32[]{:T(128)}, f32[4,4,128]{2,1,0:T(4,128)S(1)}, f32[4,4,128]{2,1,0:T(4,128)S(1)}, pred[4,4,8]{2,1,0:T(4,128)(4,1)S(1)}, bf16[4,4,128,256]{3,2,1,0...) while((s32[]{:T(128)}, f32[4,4,128]{2,1,0:T(4,128)S(1)}, ...), condition=%wide.region_6.7_spmd, body=%wide.region_3.6_spmd.sunk | while | flops 272633440 | bytes 15036589 | solution.py:73
  89.7 1.9 fusion.43
  101.8 37.1 %pmax.7 = f32[2048]{0:T(1024)S(1)} all-reduce(f32[2048]{0:T(1024)S(1)} %bitcast.148), channel_id=1, replica_groups=mesh['users'=32,'items'=16] {'items'}, use_global_device_ids=true, to_apply=%region_7.8 | all-reduce | flops 2048 | bytes 16384 | tf_op jit(solution)/shard_map/pmax | solution.py:79
  138.8 52.7 %all-reduce.1 = (f32[2048]{0:T(1024)S(1)}, f32[2048]{0:T(1024)S(1)}) all-reduce(f32[2048]{0:T(1024)S(1)} %exponential_multiply_fusion, f32[2048]{0:T(1024)S(1)} %get-tuple-element.161), channel_id=1, replica_groups=mesh['users'=32,'items'=16] {'items'}, use_global_device_ids=true, to_apply=%region_8.9 | all-reduce | flops 4096 | bytes 32768 | tf_op jit(solution)/shard_map/psum | solution.py:80
  191.6 64.0 %while.25 = (s32[]{:T(128)}, f32[8,128,256]{2,1,0:T(8,128)S(1)}, f32[4,4,128,256]{3,2,1,0:T(8,128)}, s32[4,4,8]{2,1,0:T(4,128)S(1)}, pred[4,4,8]{2,1,0:T(4,128)(...) while((s32[]{:T(128)}, f32[8,128,256]{2,1,0:T(8,128)S(1)}, ...), condition=%wide.region_12.13_spmd, body=%wide.region_10.12_spmd.sunk | while | flops 810026176 | bytes 42005372 | solution.py:112
  192.4 2.0 gather_fusion.2
  194.5 2.6 select_convert_fusion.2
  198.4 2.8 convolution_select_fusion.2
  201.2 6.4 %scatter_fusion = f32[8,128,256]{2,1,0:T(8,128)S(1)} fusion(f32[8,128,256]{2,1,0:T(8,128)S(1)} %get-tuple-element.347, s32[32]{0:T(128)S(1)} %fusion.51, f32[32,128,256]{2,1,0:T(8,128)} %bitcast.129), kind=kCustom, calls=%fused_computation.6.clone.1 | custom fusion | flops 1048576 | bytes 12583040 | tf_op jit(solution)/shard_map/while/body/eval_jaxpr/scatter-add | solution.py:99
  208.4 2.0 gather_fusion.2
  210.5 2.6 select_convert_fusion.2
  214.4 2.8 convolution_select_fusion.2
  217.2 6.5 %scatter_fusion = f32[8,128,256]{2,1,0:T(8,128)S(1)} fusion(f32[8,128,256]{2,1,0:T(8,128)S(1)} %get-tuple-element.347, s32[32]{0:T(128)S(1)} %fusion.51, f32[32,128,256]{2,1,0:T(8,128)} %bitcast.129), kind=kCustom, calls=%fused_computation.6.clone.1 | custom fusion | flops 1048576 | bytes 12583040 | tf_op jit(solution)/shard_map/while/body/eval_jaxpr/scatter-add | solution.py:99
  224.5 2.0 gather_fusion.2
  226.5 2.6 select_convert_fusion.2
  230.4 2.8 convolution_select_fusion.2
  233.2 6.5 %scatter_fusion = f32[8,128,256]{2,1,0:T(8,128)S(1)} fusion(f32[8,128,256]{2,1,0:T(8,128)S(1)} %get-tuple-element.347, s32[32]{0:T(128)S(1)} %fusion.51, f32[32,128,256]{2,1,0:T(8,128)} %bitcast.129), kind=kCustom, calls=%fused_computation.6.clone.1 | custom fusion | flops 1048576 | bytes 12583040 | tf_op jit(solution)/shard_map/while/body/eval_jaxpr/scatter-add | solution.py:99
  240.5 2.0 gather_fusion.2
  242.5 2.6 select_convert_fusion.2
  246.4 2.8 convolution_select_fusion.2
  249.2 6.5 %scatter_fusion = f32[8,128,256]{2,1,0:T(8,128)S(1)} fusion(f32[8,128,256]{2,1,0:T(8,128)S(1)} %get-tuple-element.347, s32[32]{0:T(128)S(1)} %fusion.51, f32[32,128,256]{2,1,0:T(8,128)} %bitcast.129), kind=kCustom, calls=%fused_computation.6.clone.1 | custom fusion | flops 1048576 | bytes 12583040 | tf_op jit(solution)/shard_map/while/body/eval_jaxpr/scatter-add | solution.py:99
  255.7 15.8 %scatter_custom_fusion.1 = f32[1024,256]{1,0:T(8,128)S(1)} fusion(f32[1024,256]{1,0:T(8,128)S(1)} %bitcast.128, s32[2048]{0:T(1024)S(1)} %get-tuple-element.165, bf16[2048,256]{1,0:T(8,128)(2,1)} %bitcast.137, f32[2048]{0:T(1024)S(1)} %get-tuple-element.159), kind=kCustom, calls=%fused_computation.46 | custom fusion | flops 1572864 | bytes 2105344 | tf_op jit(solution)/shard_map/scatter-add | solution.py:118
  271.5 4.4 convolution_bitcast_fusion.1
  276.0 144.6 %all-reduce.5.cloned.1.call-done = f32[1024,256]{0,1:T(8,128)} async-done(((f32[1024,256]{0,1:T(8,128)}), f32[1024,256]{0,1:T(8,128)}) %all-reduce.5.cloned.1.call-update) | async-done | bytes 1048592 | tf_op jit(solution)/shard_map/psum | solution.py:124
  420.6 3.3 fusion.17
  424.6 130.3 %all-reduce.7.cloned.1.call-done = f32[1024,256]{0,1:T(8,128)} async-done(((f32[1024,256]{0,1:T(8,128)}), f32[1024,256]{0,1:T(8,128)}) %all-reduce.7.cloned.1.call-update) | async-done | bytes 1048592 | tf_op jit(solution)/shard_map/psum | solution.py:124
  554.8 2.5 copy.14
  557.4 75.5 %reduce-scatter.2.cloned.1.call-done = f32[128,256]{1,0:T(8,128)} async-done(((f32[2048,256]{1,0:T(8,128)}), f32[128,256]{1,0:T(8,128)}) %reduce-scatter.2.cloned.1.call-update) | async-done | bytes 131088 | tf_op jit(solution)/shard_map/reduce_scatter | solution.py:114
  (137 shorter events, 31.3 us)
Async XLA Ops:
  7.2 65.9 %copy-start = (bf16[1024,256]{1,0:T(8,128)(2,1)S(1)}, bf16[1024,256]{1,0:T(8,128)(2,1)}, u32[]{:S(2)}) copy-start(bf16[1024,256]{1,0:T(8,128)(2,1)} %param.14) | copy-start | bytes 1572868
  7.2 65.9 %all-gather.2.cloned.1.call-start = ((), (), s32[]{:S(2)}) async-start(), calls=%async_computation.1 | async-start | bytes 2162688 | tf_op jit(solution)/shard_map/all_gather | solution.py:19
  7.9 412.7 %all-reduce.5.cloned.1.call-start = ((), (), s32[]{:S(2)}) async-start(), calls=%async_computation.3 | async-start | bytes 2097152 | tf_op jit(solution)/shard_map/psum | solution.py:124
  75.4 7.5 %copy-start.2 = (bf16[2048,256]{1,0:T(8,128)(2,1)S(1)}, bf16[2048,256]{1,0:T(8,128)(2,1)}, u32[]{:S(2)}) copy-start(bf16[2048,256]{1,0:T(8,128)(2,1)} %param.10) | copy-start | bytes 3145732
  82.9 1.0 copy-start.5
  82.9 0.7 copy-start.7
  87.1 1.2 copy-start.3
  91.6 1.2 copy-start.3
  96.1 1.2 copy-start.3
  100.5 1.2 copy-start.3
  192.4 2.0 copy-start.4
  194.5 2.6 copy-start.1
  208.4 2.0 copy-start.4
  210.5 2.6 copy-start.1
  224.5 2.0 copy-start.4
  226.5 2.6 copy-start.1
  240.4 2.0 copy-start.4
  242.5 2.6 copy-start.1
  275.9 144.7 %copy-start.6 = (bf16[2048,256]{1,0:T(8,128)(2,1)S(1)}, bf16[2048,256]{1,0:T(8,128)(2,1)}, u32[]{:S(2)}) copy-start(bf16[2048,256]{1,0:T(8,128)(2,1)} %copy-done.5) | copy-start | bytes 3145732
  275.9 278.9 %all-reduce.7.cloned.1.call-start = ((), (), s32[]{:S(2)}) async-start(), calls=%async_computation.4 | async-start | bytes 2097152 | tf_op jit(solution)/shard_map/psum | solution.py:124
  420.6 212.3 %reduce-scatter.2.cloned.1.call-start = ((), (), s32[]{:S(2)}) async-start(), calls=%async_computation.2 | async-start | bytes 2228224 | tf_op jit(solution)/shard_map/reduce_scatter | solution.py:114
Sparse Core Ops, SparseCore 0:
  11.1 61.8 all-gather.1
  276.1 144.4 all-reduce.4
  424.1 130.6 all-reduce.6
  558.1 74.7 reduce-scatter.1
